TPU v7x, 32 devices: a whole 2x2x4 slice. The times are simulated.
32 devices in a mesh: groups: 2 (over y), unit: 4 (over z), week: 2 (over x), region: 2 (over core).
Axes of the slice: x: 2, y: 2, z: 4, core: 2. Of those that a mesh axis runs over, the one named last changes fastest.
Arguments:
- flow_start: float32 [8, 4, 64, 8192], P(('groups', 'unit'), ('week', 'region')), parts along dimension 0, may hold values from 0 to 2
- node_start: float32 [8, 4, 64, 512], P(('groups', 'unit'), ('week', 'region')), parts along dimension 0, may hold values from -6 to 6
- seat_start: float32 [8, 64, 4096], P(('groups', 'week', 'region')), parts along dimension 0, may hold values from 0 to 4
- arc_cost: float32 [8, 4, 8192], P(('groups', 'unit'), ('week', 'region')), parts along dimension 0, may hold values from 0.05 to 25
- demand: float32 [8, 64, 4096], P(('groups', 'week', 'region')), parts along dimension 0, may hold values from 0.02 to 50
- seat_counts: float32 [8], P(('groups', 'unit')), parts along dimension 0, may hold values from 0.25 to 4
- tail_node: int32 [8, 4, 8192], P(('groups', 'unit'), ('week', 'region')), parts along dimension 0, may hold values from 0 to 511, as said below
- head_node: int32 [8, 4, 8192], P(('groups', 'unit'), ('week', 'region')), parts along dimension 0, may hold values from 0 to 511, as said below
- cover_row: int32 [8, 4, 4096], P(('groups', 'unit'), ('week', 'region')), parts along dimension 0, may hold values from 0 to 4095, as said below
Outputs:
- flows: float32 [8, 4, 64, 8192], P(('groups', 'unit'), ('week', 'region')), parts along dimension 0
- node_prices: float32 [8, 4, 64, 512], P(('groups', 'unit'), ('week', 'region')), parts along dimension 0
- seat_prices: float32 [8, 64, 4096], P(('groups', 'week', 'region')), parts along dimension 0
There are 2 independent parts, one for each index of `groups`. A program takes and returns all parts, laid end to end along the dimension named above; each array names one. Nothing has to cross between parts.
Inputs may be any that keep to these rules, and one draw needn't show every extreme that they name: `tail_node`: in each aligned block of 128 arcs of one unit type and slice, all tail nodes lie in one aligned block of 128 nodes. `head_node`: in each aligned block of 128 arcs of one unit type and slice, all head nodes lie in one aligned block of 128 nodes of the slice that holds them. `cover_row`: in each aligned block of 128 trip arcs of one unit type and slice, all rows lie in one aligned block of 128 rows.
All inputs are finite; a program needn't handle non-finite values.
Results may differ from a plain program's by a relative error of at most 0.0001.
Values sent between devices are 32-bit elements; how exact they have to be, the bound alone decides.
A program may use at most 64 MiB of HBM per device.

v0:
```python
import jax
import jax.numpy as jnp
from jax import lax
from jax.sharding import PartitionSpec as P

ITERS = 2
WRAP_ARCS = 1024
CROSS_ARCS = 1024


EPS = 1e-06
STEP = 0.5
HIGHEST = lax.Precision.HIGHEST


def from_behind(x, axis, by):
    length = lax.axis_size(axis)
    return lax.ppermute(x, axis, [(i, (i + by) % length) for i in range(length)])


def partner(block, axis, distance):
    count = lax.axis_size(axis)
    route = []
    for low in range(count):
        high = low | 1 << distance
        if high != low and high < count:
            route += [(low, high), (high, low)]
    return lax.ppermute(block, axis, route)


def block_tables(node_index, extent):
    block_count = node_index.shape[0] // 128
    grouped = node_index.reshape(block_count, 128)
    node_block = grouped[:, 0] // 128
    chooser = (node_block[:, None] == jnp.arange(extent // 128, dtype=jnp.int32)[None, :]).astype(
        jnp.float32
    )
    within_hot = (
        (grouped % 128)[:, :, None] == jnp.arange(128, dtype=jnp.int32)[None, None, :]
    ).astype(jnp.float32)
    return (chooser, within_hot)


def pick_values(field, tables):
    chooser, within_hot = tables
    columns = field.shape[0]
    tile_rows = field.reshape(columns, chooser.shape[1], 128)
    picked = jnp.einsum("smn,bm->sbn", tile_rows, chooser, precision=HIGHEST)
    gathered = jnp.einsum("sbn,bkn->sbk", picked, within_hot, precision=HIGHEST)
    return gathered.reshape(columns, -1)


def place_values(values, tables):
    chooser, within_hot = tables
    columns = values.shape[0]
    arc_tiles = values.reshape(columns, chooser.shape[0], 128)
    spread_rows = jnp.einsum("sbk,bkn->sbn", arc_tiles, within_hot, precision=HIGHEST)
    summed = jnp.einsum("sbn,bm->smn", spread_rows, chooser, precision=HIGHEST)
    return summed.reshape(columns, -1)


def local(
    flow_start,
    node_start,
    seat_start,
    arc_cost,
    demand,
    seat_counts,
    tail_node,
    head_node,
    cover_row,
):
    arc_count = flow_start.shape[3]
    node_count = node_start.shape[3]
    trip_count = seat_start.shape[2]
    trip_arcs = cover_row.shape[2]
    scenarios = flow_start.shape[2]
    cost_local = arc_cost[0, 0]
    demand_local = demand[0]
    cost_squares = jnp.sum(cost_local * cost_local)
    demand_squares = jnp.sum(demand_local * demand_local, axis=1)
    cost_total = lax.psum(cost_squares, ("unit", "week", "region"))
    demand_total = lax.psum(demand_squares, ("week", "region"))
    slice_count = lax.axis_size("week") * lax.axis_size("region")
    arcs_all = arc_count * lax.axis_size("unit") * slice_count
    trips_all = trip_count * slice_count
    weight_ratio = jnp.sqrt((cost_total / arcs_all + EPS) / (demand_total / trips_all + EPS))
    primal_step = (STEP / weight_ratio)[:, None]
    dual_step = (STEP * weight_ratio)[:, None]
    position = jnp.arange(arc_count, dtype=jnp.int32)
    arc_group = (position >= arc_count - WRAP_ARCS - CROSS_ARCS).astype(jnp.int32) + (
        position >= arc_count - CROSS_ARCS
    ).astype(jnp.int32)
    head_wide = head_node[0, 0] + arc_group * node_count
    head_tables = block_tables(head_wide, 3 * node_count)
    tail_tables = block_tables(tail_node[0, 0], node_count)
    cover_tables = block_tables(cover_row[0, 0], trip_count)
    seat_scale = seat_counts[0] / lax.axis_size("unit")
    padding = jnp.zeros((scenarios, arc_count - trip_arcs), jnp.float32)
    flow_now = flow_start[0, 0]
    prices = node_start[0, 0]
    covers = seat_start[0]
    for iteration in range(ITERS):
        prices_next = from_behind(prices, "week", -1)
        prices_other = partner(prices, "region", 0)
        extended = jnp.concatenate([prices, prices_next, prices_other], axis=1)
        head_values = pick_values(extended, head_tables)
        tail_values = pick_values(prices, tail_tables)
        cover_terms = jnp.concatenate(
            [seat_scale * pick_values(covers, cover_tables), padding], axis=1
        )
        gradient = cost_local[None, :] - cover_terms - (head_values - tail_values)
        updated = jnp.maximum(flow_now - primal_step * gradient, 0.0)
        extrapolated = 2.0 * updated - flow_now
        inflow = place_values(extrapolated, head_tables)
        outflow = place_values(extrapolated, tail_tables)
        arrived_next = from_behind(inflow[:, node_count : 2 * node_count], "week", 1)
        arrived_other = partner(inflow[:, 2 * node_count :], "region", 0)
        balance = inflow[:, :node_count] + arrived_next + arrived_other - outflow
        seat_part = place_values(seat_scale * extrapolated[:, :trip_arcs], cover_tables)
        seat_total = lax.psum(seat_part, "unit")
        covers = jnp.maximum(covers + dual_step * (demand_local - seat_total), 0.0)
        prices = prices - dual_step * balance
        flow_now = updated
    return (flow_now[None, None], prices[None, None], covers[None])


def solution(mesh):
    placed = (
        P(("groups", "unit"), ("week", "region"), None, None),
        P(("groups", "unit"), ("week", "region"), None, None),
        P(("groups", "week", "region"), None, None),
        P(("groups", "unit"), ("week", "region"), None),
        P(("groups", "week", "region"), None, None),
        P(("groups", "unit")),
        P(("groups", "unit"), ("week", "region"), None),
        P(("groups", "unit"), ("week", "region"), None),
        P(("groups", "unit"), ("week", "region"), None),
    )
    return jax.shard_map(
        local,
        mesh=mesh,
        in_specs=placed,
        out_specs=(
            P(("groups", "unit"), ("week", "region"), None, None),
            P(("groups", "unit"), ("week", "region"), None, None),
            P(("groups", "week", "region"), None, None),
        ),
        check_vma=False,
    )
```

profile of v0, /device:TPU:0, one launch (start us, length us, event | category | flops | bytes accessed | tf_op | source)
XLA Modules:
  0.0 217.3 jit_solution(6618568871857894831)
XLA Ops:
  7.7 2.6 %collective-permute-start = (f32[64,512]{1,0:T(8,128)}, f32[64,512]{1,0:T(8,128)S(1)}, u32[]{:S(2)}, u32[]{:S(2)}) collective-permute-start(f32[64,512]{1,0:T(8,128)} %bitcast.269), channel_id=1, source_target_pairs={{0,2},{2,0},{1,3},{3,1},{4,6},{6,4},{5,7},{7,5},{8,10},{10,8},{9,1... | collective-permute-start | bytes 393224 | tf_op jit(solution)/shard_map/ppermute | solution.py:18
  12.2 1.4 multiply_reduce_fusion
  14.2 33.5 %psum.28 = f32[]{:T(128)} all-reduce(f32[]{:T(128)} %multiply_reduce_fusion), channel_id=1, replica_groups=mesh['groups'=2,'unit'=4,'week'=2,'region'=2] {'unit','week','region'}, use_global_device_ids=true, to_apply=%region_1.0 | all-reduce | flops 1 | bytes 8 | tf_op jit(solution)/shard_map/psum | solution.py:82
  49.2 1.4 fusion.75
  50.6 5.8 %psum.29 = f32[64]{0:T(128)S(1)} all-reduce(f32[64]{0:T(128)S(1)} %fusion.75), channel_id=1, replica_groups=mesh['groups'=2,'unit'=4,'week'=2,'region'=2] {'week','region'}, use_global_device_ids=true, to_apply=%region_3.0 | all-reduce | flops 64 | bytes 512 | tf_op jit(solution)/shard_map/psum | solution.py:83
  58.3 3.0 %fusion.59 = f32[32,8,8,128]{3,2,1,0:T(8,128)S(1)} fusion(f32[32,64,128]{2,0,1:T(8,128)S(1)} %fusion.114, s32[32,128]{1,0:T(8,128)S(1)} %add_select_fusion.2, f32[]{:T(128)} %bitcast.3), kind=kOutput, calls=%fused_computation.64 | convolution fusion | flops 403439616 | bytes 2113540 | tf_op jit(solution)/shard_map/sbn,bkn->sbk/dot_general | solution.py:49
  63.0 6.0 %fusion.3 = f32[64,128,64]{1,2,0:T(8,128)} fusion(f32[64,64,128]{2,0,1:T(8,128)S(1)} %fusion.139, s32[64,128]{1,0:T(8,128)S(1)} %copy.27), kind=kOutput, calls=%fused_computation.4 | convolution fusion | flops 806354944 | bytes 4227072 | tf_op jit(solution)/shard_map/sbn,bkn->sbk/dot_general | solution.py:49
  70.8 5.9 %subtract_bitcast_fusion.1 = f32[64,8,8,128]{3,2,1,0:T(8,128)S(1)} fusion(f32[64,128,64]{1,2,0:T(8,128)S(1)} %copy-done.8, f32[64,64,128]{2,0,1:T(8,128)S(1)} %fusion.89, s32[64,128]{1,0:T(8,128)S(1)} %copy.23), kind=kOutput, calls=%fused_computation.45 | convolution fusion | flops 806879232 | bytes 6324224 | tf_op jit(solution)/shard_map/sbn,bkn->sbk/dot_general | solution.py:49
  78.0 2.0 fusion.48
  80.0 4.0 %fusion.2 = f32[64,128,64]{1,2,0:T(8,128)S(1)} fusion(s32[64,128]{1,0:T(8,128)S(1)} %copy.27, f32[64,8192]{1,0:T(8,128)S(1)} %bitcast_subtract_fusion.2), kind=kOutput, calls=%fused_computation.3 | convolution fusion | flops 806354944 | bytes 4227072 | tf_op jit(solution)/shard_map/sbk,bkn->sbn/dot_general | solution.py:57
  84.0 4.0 %fusion.6 = f32[64,128,64]{1,2,0:T(8,128)} fusion(s32[64,128]{1,0:T(8,128)S(1)} %copy.23, f32[64,8192]{1,0:T(8,128)S(1)} %bitcast_subtract_fusion.2), kind=kOutput, calls=%fused_computation.8 | convolution fusion | flops 806354944 | bytes 4227072 | tf_op jit(solution)/shard_map/sbk,bkn->sbn/dot_general | solution.py:57
  88.0 1.3 fusion.71
  89.3 1.6 copy.162
  91.1 3.4 %fusion.26 = f32[12,64,128]{2,0,1:T(8,128)S(1)} fusion(f32[64,128,64]{1,2,0:T(8,128)} %fusion.6, s32[64]{0:T(128)S(1)} %fusion.132), kind=kOutput, calls=%fused_computation.30 | convolution fusion | flops 75498240 | bytes 2490624 | tf_op jit(solution)/shard_map/sbn,bm->smn/dot_general | solution.py:58
  94.9 2.0 fusion.24
  96.8 3.1 %collective-permute-done.2 = f32[64,512]{1,0:T(8,128)S(1)} collective-permute-done((f32[64,512]{1,0:T(8,128)S(1)}, f32[64,512]{1,0:T(8,128)S(1)}, u32[]{:S(2)}, u32[]{:S(2)}) %collective-permute-start.2) | collective-permute-done | bytes 131104 | tf_op jit(solution)/shard_map/ppermute | solution.py:18
  101.7 6.0 %fusion.1 = f32[64,128,64]{1,2,0:T(8,128)} fusion(f32[64,64,128]{2,0,1:T(8,128)S(1)} %fusion.136, s32[64,128]{1,0:T(8,128)S(1)} %copy.27), kind=kOutput, calls=%fused_computation.2 | convolution fusion | flops 806354944 | bytes 4227072 | tf_op jit(solution)/shard_map/sbn,bkn->sbk/dot_general | solution.py:49
  109.4 6.0 %subtract_bitcast_fusion = f32[64,8,8,128]{3,2,1,0:T(8,128)} fusion(f32[64,128,64]{1,2,0:T(8,128)S(1)} %copy-done.9, f32[64,64,128]{2,0,1:T(8,128)S(1)} %fusion.122, s32[64,128]{1,0:T(8,128)S(1)} %copy.23), kind=kOutput, calls=%fused_computation.44 | convolution fusion | flops 806879232 | bytes 6324224 | tf_op jit(solution)/shard_map/sbn,bkn->sbk/dot_general | solution.py:49
  115.4 24.7 %all-reduce.5.cloned.1.call-done = f32[64,4096]{1,0:T(8,128)} async-done(((f32[64,4096]{1,0:T(8,128)}), f32[64,4096]{1,0:T(8,128)}) %all-reduce.5.cloned.1.call-update) | async-done | bytes 1048592 | tf_op jit(solution)/shard_map/psum | solution.py:121
  140.1 1.4 fusion.107
  142.5 3.0 %fusion.61 = f32[32,8,8,128]{3,2,1,0:T(8,128)S(1)} fusion(f32[32,64,128]{2,0,1:T(8,128)S(1)} %fusion.111, s32[32,128]{1,0:T(8,128)S(1)} %add_select_fusion.2, f32[]{:T(128)} %bitcast.3), kind=kOutput, calls=%fused_computation.66 | convolution fusion | flops 403439616 | bytes 2113540 | tf_op jit(solution)/shard_map/sbn,bkn->sbk/dot_general | solution.py:49
  145.6 2.1 multiply_subtract_fusion
  147.7 2.0 fusion.46
  149.7 4.0 %fusion.4 = f32[64,128,64]{1,2,0:T(8,128)} fusion(s32[64,128]{1,0:T(8,128)S(1)} %copy.23, f32[64,8192]{1,0:T(8,128)S(1)} %get-tuple-element.5), kind=kOutput, calls=%fused_computation.6 | convolution fusion | flops 806354944 | bytes 4227072 | tf_op jit(solution)/shard_map/sbk,bkn->sbn/dot_general | solution.py:57
  153.7 1.3 fusion.68
  155.0 1.6 copy.161
  156.6 3.4 %fusion.20 = f32[12,64,128]{2,0,1:T(8,128)S(1)} fusion(f32[64,128,64]{1,2,0:T(8,128)} %fusion.4, s32[64]{0:T(128)S(1)} %fusion.132), kind=kOutput, calls=%fused_computation.24 | convolution fusion | flops 75498240 | bytes 2490624 | tf_op jit(solution)/shard_map/sbn,bm->smn/dot_general | solution.py:58
  160.2 1.5 collective-permute-start.6
  161.7 4.2 %fusion = f32[64,128,64]{1,2,0:T(8,128)S(1)} fusion(s32[64,128]{1,0:T(8,128)S(1)} %copy.27, f32[64,8192]{1,0:T(8,128)S(1)} %get-tuple-element.5), kind=kOutput, calls=%fused_computation.1 | convolution fusion | flops 806354944 | bytes 4227072 | tf_op jit(solution)/shard_map/sbk,bkn->sbn/dot_general | solution.py:57
  166.0 2.0 fusion.18
  168.7 39.3 %all-reduce.7.cloned.1.call-done = f32[64,4096]{1,0:T(8,128)} async-done(((f32[64,4096]{1,0:T(8,128)}), f32[64,4096]{1,0:T(8,128)}) %all-reduce.7.cloned.1.call-update) | async-done | bytes 1048592 | tf_op jit(solution)/shard_map/psum | solution.py:121
  208.0 2.5 %fusion.80 = f32[1,64,4096]{2,1,0:T(8,128)} fusion(f32[64,4096]{1,0:T(8,128)} %all-reduce.7.cloned.1.call-done, f32[1,64,4096]{2,1,0:T(8,128)S(1)} %copy-done.4, f32[64]{0:T(128)S(1)} %get-tuple-element.3, f32[64,4096]{1,0:T(8,128)S(1)} %copy-done.12, f32[1,64,4096]{2,1,0:T(8,128)S(1)} %copy-done.2), kind=kLoop, calls=%fused_computation.95 | loop fusion | flops 2097152 | bytes 5243136 | tf_op jit(solution)/shard_map/broadcast_in_dim | solution.py:125
  (83 shorter events, 15.6 us)
Async XLA Ops:
  7.2 50.3 %copy-start.2 = (f32[1,64,4096]{2,1,0:T(8,128)S(1)}, f32[1,64,4096]{2,1,0:T(8,128)}, u32[]{:S(2)}) copy-start(f32[1,64,4096]{2,1,0:T(8,128)} %param.11) | copy-start | bytes 3145732
  7.2 133.0 %all-reduce.5.cloned.1.call-start = ((), (), s32[]{:S(2)}) async-start(), calls=%async_computation | async-start | bytes 2097152 | tf_op jit(solution)/shard_map/psum | solution.py:121
  7.2 61.8 %collective-permute-start.1 = (f32[64,512]{1,0:T(8,128)}, f32[64,512]{1,0:T(8,128)S(1)}, u32[]{:S(2)}, u32[]{:S(2)}) collective-permute-start(f32[64,512]{1,0:T(8,128)} %bitcast.268), channel_id=1, source_target_pairs={{0,1},{1,0},{2,3},{3,2},{4,5},{5,4},{6,7},{7,6},{8,9},{9,8},{10,11... | collective-permute-start | bytes 393224 | tf_op jit(solution)/shard_map/ppermute | solution.py:28
  7.7 61.4 %collective-permute-start = (f32[64,512]{1,0:T(8,128)}, f32[64,512]{1,0:T(8,128)S(1)}, u32[]{:S(2)}, u32[]{:S(2)}) collective-permute-start(f32[64,512]{1,0:T(8,128)} %bitcast.269), channel_id=1, source_target_pairs={{0,2},{2,0},{1,3},{3,1},{4,6},{6,4},{5,7},{7,5},{8,10},{10,8},{9,1... | collective-permute-start | bytes 393224 | tf_op jit(solution)/shard_map/ppermute | solution.py:18
  61.3 15.3 %copy-start.5 = (f32[32,8,8,128]{3,2,0,1:T(8,128)}, f32[32,8,8,128]{3,2,0,1:T(8,128)S(1)}, u32[]{:S(2)}) copy-start(f32[32,8,8,128]{3,2,0,1:T(8,128)S(1)} %copy.164) | copy-start | bytes 3145732
  69.2 1.6 copy-start.8
  70.8 5.9 %copy-start.10 = (f32[1,1,64,8192]{3,2,1,0:T(8,128)S(1)}, f32[1,1,64,8192]{3,2,1,0:T(8,128)}, u32[]{:S(2)}) copy-start(f32[1,1,64,8192]{3,2,1,0:T(8,128)} %param.9) | copy-start | bytes 6291460
  70.8 5.9 %copy-start.14 = (f32[1,1,8192]{2,1,0:T(1,128)S(1)}, f32[1,1,8192]{2,1,0:T(1,128)}, u32[]{:S(2)}) copy-start(f32[1,1,8192]{2,1,0:T(1,128)} %param.12) | copy-start | bytes 98308
  76.6 1.3 copy-start
  90.9 117.1 %all-reduce.7.cloned.1.call-start = ((), (), s32[]{:S(2)}) async-start(), calls=%async_computation.1 | async-start | bytes 2097152 | tf_op jit(solution)/shard_map/psum | solution.py:121
  94.6 5.4 %copy-start.13 = (f32[1,1,64,512]{3,2,1,0:T(8,128)S(1)}, f32[1,1,64,512]{3,2,1,0:T(8,128)}, u32[]{:S(2)}) copy-start(f32[1,1,64,512]{3,2,1,0:T(8,128)} %param.10) | copy-start | bytes 393220
  94.7 5.2 %collective-permute-start.2 = (f32[64,512]{1,0:T(8,128)S(1)}, f32[64,512]{1,0:T(8,128)S(1)}, u32[]{:S(2)}, u32[]{:S(2)}) collective-permute-start(f32[64,512]{1,0:T(8,128)S(1)} %get-tuple-element.9), channel_id=1, source_target_pairs={{0,2},{2,0},{1,3},{3,1},{4,6},{6,4},{5,7},{7,5},{8,10},{10,8},{9,1... | collective-permute-start | bytes 393224 | tf_op jit(solution)/shard_map/ppermute | solution.py:18
  94.8 5.2 %collective-permute-start.3 = (f32[64,512]{1,0:T(8,128)S(1)}, f32[64,512]{1,0:T(8,128)S(1)}, u32[]{:S(2)}, u32[]{:S(2)}) collective-permute-start(f32[64,512]{1,0:T(8,128)S(1)} %get-tuple-element.10), channel_id=1, source_target_pairs={{0,1},{1,0},{2,3},{3,2},{4,5},{5,4},{6,7},{7,6},{8,9},{9,8},{10,11... | collective-permute-start | bytes 393224 | tf_op jit(solution)/shard_map/ppermute | solution.py:28
  100.1 7.6 %collective-permute-start.5 = (f32[64,512]{1,0:T(8,128)S(1)}, f32[64,512]{1,0:T(8,128)S(1)}, u32[]{:S(2)}, u32[]{:S(2)}) collective-permute-start(f32[64,512]{1,0:T(8,128)S(1)} %fusion.100), channel_id=1, source_target_pairs={{0,1},{1,0},{2,3},{3,2},{4,5},{5,4},{6,7},{7,6},{8,9},{9,8},{10,11... | collective-permute-start | bytes 393224 | tf_op jit(solution)/shard_map/ppermute | solution.py:28
  100.2 7.5 %collective-permute-start.4 = (f32[64,512]{1,0:T(8,128)S(1)}, f32[64,512]{1,0:T(8,128)S(1)}, u32[]{:S(2)}, u32[]{:S(2)}) collective-permute-start(f32[64,512]{1,0:T(8,128)S(1)} %fusion.100), channel_id=1, source_target_pairs={{0,2},{2,0},{1,3},{3,1},{4,6},{6,4},{5,7},{7,5},{8,10},{10,8},{9,1... | collective-permute-start | bytes 393224 | tf_op jit(solution)/shard_map/ppermute | solution.py:18
  107.8 1.6 copy-start.9
  109.4 30.7 %copy-start.3 = (f32[1,64,4096]{2,1,0:T(8,128)S(1)}, f32[1,64,4096]{2,1,0:T(8,128)}, u32[]{:S(2)}) copy-start(f32[1,64,4096]{2,1,0:T(8,128)} %param.13) | copy-start | bytes 3145732
  141.6 3.9 %copy-start.11 = (f32[1,1,64,8192]{3,2,1,0:T(8,128)S(1)}, f32[1,1,64,8192]{3,2,1,0:T(8,128)}, u32[]{:S(2)}) copy-start(f32[1,1,64,8192]{3,2,1,0:T(8,128)} %param.9) | copy-start | bytes 6291460
  141.8 3.7 %copy-start.7 = (f32[64,8,8,128]{3,2,1,0:T(8,128)S(1)}, f32[64,8,8,128]{3,2,1,0:T(8,128)}, u32[]{:S(2)}) copy-start(f32[64,8,8,128]{3,2,1,0:T(8,128)} %subtract_bitcast_fusion) | copy-start | bytes 6291460
  142.5 3.1 %copy-start.1 = (f32[64,8,8,128]{3,2,1,0:T(8,128)S(1)}, f32[64,8,8,128]{3,2,1,0:T(8,128)}, u32[]{:S(2)}) copy-start(f32[64,8,8,128]{3,2,1,0:T(8,128)} %copy-done) | copy-start | bytes 6291460
  142.5 3.1 %copy-start.6 = (f32[32,8,8,128]{3,2,0,1:T(8,128)S(1)}, f32[32,8,8,128]{3,2,0,1:T(8,128)}, u32[]{:S(2)}) copy-start(f32[32,8,8,128]{3,2,0,1:T(8,128)} %copy-done.5) | copy-start | bytes 3145732
  160.2 7.7 %collective-permute-start.6 = (f32[64,512]{1,0:T(8,128)S(1)}, f32[64,512]{1,0:T(8,128)S(1)}, u32[]{:S(2)}, u32[]{:S(2)}) collective-permute-start(f32[64,512]{1,0:T(8,128)S(1)} %get-tuple-element.7), channel_id=1, source_target_pairs={{0,2},{2,0},{1,3},{3,1},{4,6},{6,4},{5,7},{7,5},{8,10},{10,8},{9,1... | collective-permute-start | bytes 393224 | tf_op jit(solution)/shard_map/ppermute | solution.py:18
  161.7 6.2 %collective-permute-start.7 = (f32[64,512]{1,0:T(8,128)S(1)}, f32[64,512]{1,0:T(8,128)S(1)}, u32[]{:S(2)}, u32[]{:S(2)}) collective-permute-start(f32[64,512]{1,0:T(8,128)S(1)} %get-tuple-element.8), channel_id=1, source_target_pairs={{0,1},{1,0},{2,3},{3,2},{4,5},{5,4},{6,7},{7,6},{8,9},{9,8},{10,11... | collective-permute-start | bytes 393224 | tf_op jit(solution)/shard_map/ppermute | solution.py:28
  166.0 42.0 %copy-start.4 = (f32[1,64,4096]{2,1,0:T(8,128)S(1)}, f32[1,64,4096]{2,1,0:T(8,128)}, u32[]{:S(2)}) copy-start(f32[1,64,4096]{2,1,0:T(8,128)} %param.13) | copy-start | bytes 3145732
  166.0 42.0 %copy-start.12 = (f32[64,4096]{1,0:T(8,128)S(1)}, f32[64,4096]{1,0:T(8,128)}, u32[]{:S(2)}) copy-start(f32[64,4096]{1,0:T(8,128)} %all-reduce.5.cloned.1.call-done) | copy-start | bytes 3145732
Sparse Core Ops, SparseCore 0:
  91.0 49.1 all-reduce.4
  156.7 51.1 all-reduce.6
where the time goes:
time: 218 us; the launch traced here: 217 us
  matrix products  68.8 us (32%)
  waiting for transfers between devices  67.2 us (31%)
  blocking collectives  39.2 us (18%)
  between operations  15.9 us (7%)
  other arithmetic  11.1 us (5%)
  local copies, waits for them, and re-layouts  9.64 us (4%)
  starting transfers between devices  5.55 us (3%)
    psum x2, waiting for transfers between devices, local(): seat_total = lax.psum(seat_part, 'unit')  64 us
    psum x1, blocking collectives, local(): cost_total = lax.psum(cost_squares, ('unit', 'week', 'region'))  33.5 us
    dot_general x6, matrix products, pick_values(): gathered = jnp.einsum('sbn,bkn->sbk', picked, within_hot, precision=HIGHEST)  29.8 us
    dot_general x6, matrix products, place_values(): jnp.einsum('sbk,bkn->sbn', arc_tiles, within_hot, precision=HIGHEST)  20.2 us
    dot_general x6, matrix products, place_values(): summed = jnp.einsum('sbn,bm->smn', spread_rows, chooser, precision=HIGHEST)  13.4 us
    unnamed x37, local copies, waits for them, and re-layouts  6.46 us
    psum x1, blocking collectives, local(): demand_total = lax.psum(demand_squares, ('week', 'region'))  5.76 us
    dot_general x6, matrix products, pick_values(): picked = jnp.einsum('smn,bm->sbn', tile_rows, chooser, precision=HIGHEST)  5.4 us
  transfers between devices with their start and end apart: 10, of which 3 were waited for; matrix products, arithmetic and copies ran while one was open for 22% of the time, Pallas kernels for 0%

commit v1 on v0

v1 whole, which is shorter than its diff:
```python
import functools

import jax
import jax.numpy as jnp
from jax import lax
from jax.experimental import pallas as pl
from jax.experimental.pallas import tpu as pltpu
from jax.sharding import PartitionSpec as P

ITERS = 2
WRAP_ARCS = 1024
CROSS_ARCS = 1024
EPS = 1e-06
STEP = 0.5
CHUNKS = 4
UNROLL = 8
MESH = pl.DeviceIdType.MESH
F32 = jnp.float32
BF16 = jnp.bfloat16


def split_rows(value):
    high = value.astype(BF16)
    low = (value - high.astype(F32)).astype(BF16)
    return jnp.concatenate([high, low], axis=0)


def pick(block, index):
    return jnp.take_along_axis(block, index, axis=1, mode="promise_in_bounds")


def kernel(
    units, weeks, chunks,
    flow_ref, node_ref, seat_ref, cost_ref, demand_ref, count_ref, tail_ref, head_ref, cover_ref,
    meta_ref,
    flow_out, node_out, seat_out,
    hot_ends, hot_cover, covers, price_local, chain, own_price, recv_price, own_balance, send_in,
    recv_in, part, send_right, send_left, recv_right, recv_left, stat_mine, stat_slices, cost_mine,
    cost_units, primal, dual,
    stat_send, stat_recv, unit_send, unit_recv, price_send, price_recv, in_send, in_recv,
    right_send, right_recv, left_send, left_recv,
):
    me = lax.axis_index("unit")
    week = lax.axis_index("week")
    region = lax.axis_index("region")
    scen, arcs = flow_ref.shape
    nodes = node_ref.shape[1]
    trips = seat_ref.shape[1]
    rows = scen // chunks
    node_blocks = nodes // 128
    trip_blocks = trips // 128
    arc_blocks = arcs // 128
    cover_blocks = cover_ref.shape[0]
    slices = 2 * weeks
    mine = week * 2 + region
    ahead = lax.rem(week + 1, weeks)
    behind = lax.rem(week + weeks - 1, weeks)
    stride = max(chunks, units - 1)
    scale = count_ref[0] / units

    barrier = pltpu.get_barrier_semaphore()
    for step in range(1, units):
        other = lax.rem(me + step, units)
        pl.semaphore_signal(barrier, inc=1, device_id={"unit": other}, device_id_type=MESH)
    for step in range(1, slices):
        other = lax.rem(mine + step, slices)
        pl.semaphore_signal(
            barrier, inc=1, device_id={"week": other // 2, "region": other % 2},
            device_id_type=MESH,
        )

    demand_squares = jnp.zeros((scen, 128), F32)
    for block in range(trip_blocks):
        piece = demand_ref[:, block * 128 : block * 128 + 128]
        demand_squares += piece * piece
    cost_squares = jnp.zeros((8, 128), F32)
    for block in range(arc_blocks // 8):
        piece = cost_ref[block * 8 : block * 8 + 8, :]
        cost_squares += piece * piece
    stat_mine[0:scen, :] = demand_squares
    stat_mine[scen : scen + 8, :] = cost_squares
    for c in range(chunks):
        for block in range(node_blocks):
            own_price[c, block] = node_ref[
                c * rows : c * rows + rows, block * 128 : block * 128 + 128
            ]
    pl.semaphore_wait(barrier, units - 1 + slices - 1)

    def stat_copy(other, slot):
        return pltpu.make_async_remote_copy(
            src_ref=stat_mine, dst_ref=stat_slices.at[slot], send_sem=stat_send.at[other],
            recv_sem=stat_recv.at[slot],
            device_id={"week": other // 2, "region": other % 2}, device_id_type=MESH,
        )

    def unit_copy(other, slot):
        return pltpu.make_async_remote_copy(
            src_ref=cost_mine, dst_ref=cost_units.at[slot], send_sem=unit_send.at[other],
            recv_sem=unit_recv.at[slot], device_id={"unit": other}, device_id_type=MESH,
        )

    def price_copy(side, item):
        target = {"week": behind} if side == 0 else {"region": 1 - region}
        return pltpu.make_async_remote_copy(
            src_ref=own_price.at[item], dst_ref=recv_price.at[side, item],
            send_sem=price_send.at[side, item], recv_sem=price_recv.at[side, item],
            device_id=target, device_id_type=MESH,
        )

    def in_copy(side, item):
        target = {"week": ahead} if side == 0 else {"region": 1 - region}
        return pltpu.make_async_remote_copy(
            src_ref=send_in.at[side, item], dst_ref=recv_in.at[side, item],
            send_sem=in_send.at[side, item], recv_sem=in_recv.at[side, item],
            device_id=target, device_id_type=MESH,
        )

    def right_copy(item):
        return pltpu.make_async_remote_copy(
            src_ref=send_right.at[item], dst_ref=recv_right.at[item],
            send_sem=right_send.at[item], recv_sem=right_recv.at[item],
            device_id={"unit": lax.rem(me + 1, units)}, device_id_type=MESH,
        )

    def left_copy(item):
        return pltpu.make_async_remote_copy(
            src_ref=send_left.at[item], dst_ref=recv_left.at[item],
            send_sem=left_send.at[item], recv_sem=left_recv.at[item],
            device_id={"unit": lax.rem(me + units - 1, units)}, device_id_type=MESH,
        )

    for step in range(1, slices):
        stat_copy(lax.rem(mine + step, slices), mine).start()
    for c in range(chunks):
        price_copy(0, c).start()
        price_copy(1, c).start()

    sub = lax.broadcasted_iota(jnp.int32, (128, 128), 0)

    def hot(row):
        return jnp.where(jnp.broadcast_to(row, (128, 128)) == sub, 1.0, 0.0).astype(BF16)

    @pl.loop(0, arc_blocks // 8)
    def _(group):
        at = pl.ds(pl.multiple_of(group * 8, 8), 8)
        heads = head_ref[at, :] & 127
        tails = tail_ref[at, :] & 127
        for k in range(8):
            hot_ends[group * 8 + k, 0:128, :] = hot(heads[k : k + 1, :])
            hot_ends[group * 8 + k, 128:256, :] = hot(tails[k : k + 1, :])

    @pl.loop(0, cover_blocks // 8)
    def _(group):
        at = pl.ds(pl.multiple_of(group * 8, 8), 8)
        targets = cover_ref[at, :] & 127
        for k in range(8):
            hot_cover[group * 8 + k] = hot(targets[k : k + 1, :])

    for c in range(chunks):
        for block in range(trip_blocks):
            covers[c * trip_blocks + block] = seat_ref[
                c * rows : c * rows + rows, block * 128 : block * 128 + 128
            ]
    flow_out[...] = flow_ref[...]
    chain[0] = jnp.zeros((rows, 128), F32)

    @pl.when(me == 0)
    def _():
        recv_right[...] = jnp.zeros_like(recv_right)

    @pl.when(me == units - 1)
    def _():
        recv_left[...] = jnp.zeros_like(recv_left)

    for step in range(1, slices):
        stat_copy(mine, lax.rem(mine + step, slices)).wait_recv()
    stat_total = stat_mine[...]
    for step in range(1, slices):
        stat_total += stat_slices[lax.rem(mine + step, slices)]
    cost_mine[...] = stat_total[scen : scen + 8, :]
    for step in range(1, units):
        unit_copy(lax.rem(me + step, units), me).start()
    for step in range(1, units):
        unit_copy(me, lax.rem(me + step, units)).wait_recv()
    cost_total = cost_mine[...]
    for step in range(1, units):
        cost_total += cost_units[lax.rem(me + step, units)]
    cost_sum = jnp.sum(jnp.sum(cost_total, axis=0, keepdims=True), axis=1, keepdims=True)
    demand_sum = jnp.sum(stat_total[0:scen, :], axis=1, keepdims=True)
    ratio = jnp.sqrt(
        (cost_sum / (arcs * units * slices) + EPS) / (demand_sum / (trips * slices) + EPS)
    )
    primal[...] = jnp.broadcast_to(STEP / ratio, (scen, 128))
    dual[...] = jnp.broadcast_to(STEP * ratio, (scen, 128))

    head_at, tail_at = 0, arc_blocks
    cover_at = 2 * arc_blocks
    prev_at = cover_at + cover_blocks
    last_at = prev_at + cover_blocks
    cross = arc_blocks - CROSS_ARCS // 128
    wrap = cross - WRAP_ARCS // 128

    def compute(item, c):
        there = pl.ds(pl.multiple_of(c * rows, 8), rows)
        price_copy(0, item).wait_recv()
        price_copy(1, item).wait_recv()
        price_local[0:node_blocks] = own_price[item]
        price_local[node_blocks : 2 * node_blocks] = recv_price[0, item]
        price_local[2 * node_blocks : 3 * node_blocks] = recv_price[1, item]
        step_size = primal[there, :]

        def section(first, end, side, with_cover, start):
            def body(group, carry):
                own, away = list(carry[0]), list(carry[1])
                base = first + group * UNROLL
                at = pl.ds(pl.multiple_of(base, 8), UNROLL)
                heads = head_ref[at, :] & 127
                tails = tail_ref[at, :] & 127
                costs = cost_ref[at, :]
                if with_cover:
                    targets = cover_ref[at, :] & 127
                for k in range(UNROLL):
                    b = base + k
                    head_block = meta_ref[head_at + b]
                    tail_block = meta_ref[tail_at + b]
                    head_value = pick(
                        price_local[side * node_blocks + head_block],
                        jnp.broadcast_to(heads[k : k + 1, :], (rows, 128)),
                    )
                    tail_value = pick(
                        price_local[tail_block],
                        jnp.broadcast_to(tails[k : k + 1, :], (rows, 128)),
                    )
                    gradient = jnp.broadcast_to(costs[k : k + 1, :], (rows, 128))
                    if with_cover:
                        seat = pick(
                            covers[c * trip_blocks + meta_ref[cover_at + b]],
                            jnp.broadcast_to(targets[k : k + 1, :], (rows, 128)),
                        )
                        gradient = gradient - scale * seat
                    gradient = gradient - (head_value - tail_value)
                    column = pl.ds(pl.multiple_of(b * 128, 128), 128)
                    now = flow_out[there, column]
                    updated = jnp.maximum(now - step_size * gradient, 0.0)
                    flow_out[there, column] = updated
                    halves = split_rows(2.0 * updated - now)
                    ends = lax.dot_general(
                        halves, hot_ends[b], (((1,), (1,)), ((), ())),
                        preferred_element_type=F32,
                    )
                    ends = ends[0:rows] + ends[rows : 2 * rows]
                    into, outof = ends[:, 0:128], ends[:, 128:256]
                    for m in range(node_blocks):
                        landed = jnp.where(head_block == m, into, 0.0)
                        left = jnp.where(tail_block == m, outof, 0.0)
                        if side == 0:
                            own[m] = own[m] + (landed - left)
                        else:
                            own[m] = own[m] - left
                            away[m] = away[m] + landed
                    if with_cover:
                        filled = lax.dot_general(
                            halves, hot_cover[b], (((1,), (1,)), ((), ())),
                            preferred_element_type=F32,
                        )
                        filled = filled[0:rows] + filled[rows : 2 * rows]
                        chain[b + 1] = scale * filled + chain[meta_ref[prev_at + b]]
                return tuple(own), tuple(away)

            return lax.fori_loop(0, (end - first) // UNROLL, body, start)

        zeros = tuple(jnp.zeros((rows, 128), F32) for _ in range(node_blocks))
        own, _ = section(0, cover_blocks, 0, True, (zeros, ()))
        own, _ = section(cover_blocks, wrap, 0, False, (own, ()))
        own, away_next = section(wrap, cross, 1, False, (own, zeros))
        own, away_other = section(cross, arc_blocks, 2, False, (own, zeros))
        for m in range(node_blocks):
            own_balance[item, m] = own[m]
            send_in[0, item, m] = away_next[m]
            send_in[1, item, m] = away_other[m]
        in_copy(0, item).start()
        in_copy(1, item).start()
        for m in range(trip_blocks):
            part[item, m] = chain[meta_ref[last_at + m]]

    def settle_nodes(item, c, it):
        there = pl.ds(pl.multiple_of(c * rows, 8), rows)
        in_copy(0, item).wait_recv()
        in_copy(1, item).wait_recv()
        step_size = dual[there, :]

        def priced(m):
            balance = own_balance[item, m] + recv_in[0, item, m] + recv_in[1, item, m]
            return own_price[item, m] - step_size * balance

        @pl.when(it < ITERS - 1)
        def _():
            for m in range(node_blocks):
                own_price[item + chunks, m] = priced(m)
            price_copy(0, item + chunks).start()
            price_copy(1, item + chunks).start()

        @pl.when(it == ITERS - 1)
        def _():
            for m in range(node_blocks):
                node_out[there, m * 128 : m * 128 + 128] = priced(m)

    def settle_seats(item, c, it):
        there = pl.ds(pl.multiple_of(c * rows, 8), rows)
        step_size = dual[there, :]

        def covered(m):
            total = recv_right[item, m] + part[item, m] + recv_left[item, m]
            wanted = demand_ref[there, m * 128 : m * 128 + 128]
            return jnp.maximum(
                covers[c * trip_blocks + m] + step_size * (wanted - total), 0.0
            )

        @pl.when(it < ITERS - 1)
        def _():
            for m in range(trip_blocks):
                covers[c * trip_blocks + m] = covered(m)

        @pl.when(it == ITERS - 1)
        def _():
            for m in range(trip_blocks):
                seat_out[there, m * 128 : m * 128 + 128] = covered(m)

    def at_slot(slot, action):
        it = slot // stride
        c = slot % stride

        @pl.when((slot >= 0) & (c < chunks) & (it < ITERS))
        def _():
            action(it * chunks + c, c, it)

    def forward_right(item, c, it):
        @pl.when(me > 0)
        def _():
            right_copy(item).wait_recv()

        @pl.when(me < units - 1)
        def _():
            send_right[item] = part[item] + recv_right[item]
            right_copy(item).start()

    def forward_left(item, c, it):
        @pl.when(me < units - 1)
        def _():
            left_copy(item).wait_recv()

        @pl.when(me > 0)
        def _():
            send_left[item] = part[item] + recv_left[item]
            left_copy(item).start()

    far = jnp.maximum(me, units - 1 - me)

    @pl.loop(0, (ITERS - 1) * stride + chunks + units - 1)
    def _(slot):
        at_slot(slot, lambda item, c, it: compute(item, c))
        at_slot(slot - me, forward_right)
        at_slot(slot - (units - 1 - me), forward_left)
        at_slot(slot, settle_nodes)
        at_slot(slot - far, settle_seats)

    for step in range(1, slices):
        stat_copy(lax.rem(mine + step, slices), mine).wait_send()
    for step in range(1, units):
        unit_copy(lax.rem(me + step, units), me).wait_send()

    @pl.loop(0, ITERS * chunks)
    def _(item):
        for side in range(2):
            price_copy(side, item).wait_send()
            in_copy(side, item).wait_send()

        @pl.when(me < units - 1)
        def _():
            right_copy(item).wait_send()

        @pl.when(me > 0)
        def _():
            left_copy(item).wait_send()


def local(
    units, weeks, flow_start, node_start, seat_start, arc_cost, demand, seat_counts, tail_node,
    head_node, cover_row,
):
    scen, arcs = flow_start.shape[2:]
    nodes = node_start.shape[3]
    trips = seat_start.shape[2]
    node_blocks, trip_blocks, arc_blocks = nodes // 128, trips // 128, arcs // 128
    cover_blocks = cover_row.shape[2] // 128
    heads = head_node.reshape(arc_blocks, 128)
    tails = tail_node.reshape(arc_blocks, 128)
    targets = cover_row.reshape(cover_blocks, 128)
    target_block = targets[:, 0] // 128
    order = jnp.arange(cover_blocks, dtype=jnp.int32)
    same = target_block[:, None] == target_block[None, :]
    earlier = order[None, :] < order[:, None]
    previous = jnp.max(jnp.where(same & earlier, order[None, :] + 1, 0), axis=1)
    wanted = jnp.arange(trip_blocks, dtype=jnp.int32)[:, None] == target_block[None, :]
    last = jnp.max(jnp.where(wanted, order[None, :] + 1, 0), axis=1)
    meta = jnp.concatenate([heads[:, 0] // 128, tails[:, 0] // 128, target_block, previous, last])

    chunks = CHUNKS
    rows = scen // chunks
    items = ITERS * chunks
    slices = 2 * weeks
    vmem = pl.BlockSpec(memory_space=pltpu.VMEM)
    smem = pl.BlockSpec(memory_space=pltpu.SMEM)
    dma = pltpu.SemaphoreType.DMA
    flows, prices, seats = pl.pallas_call(
        functools.partial(kernel, units, weeks, chunks),
        out_shape=(
            jax.ShapeDtypeStruct((scen, arcs), F32),
            jax.ShapeDtypeStruct((scen, nodes), F32),
            jax.ShapeDtypeStruct((scen, trips), F32),
        ),
        in_specs=[vmem, vmem, vmem, vmem, vmem, smem, vmem, vmem, vmem, smem],
        out_specs=(vmem, vmem, vmem),
        scratch_shapes=[
            pltpu.VMEM((arc_blocks, 256, 128), BF16),
            pltpu.VMEM((cover_blocks, 128, 128), BF16),
            pltpu.VMEM((chunks * trip_blocks, rows, 128), F32),
            pltpu.VMEM((3 * node_blocks, rows, 128), F32),
            pltpu.VMEM((cover_blocks + 1, rows, 128), F32),
            pltpu.VMEM((items, node_blocks, rows, 128), F32),
            pltpu.VMEM((2, items, node_blocks, rows, 128), F32),
            pltpu.VMEM((items, node_blocks, rows, 128), F32),
            pltpu.VMEM((2, items, node_blocks, rows, 128), F32),
            pltpu.VMEM((2, items, node_blocks, rows, 128), F32),
        ]
        + [pltpu.VMEM((items, trip_blocks, rows, 128), F32)] * 5
        + [
            pltpu.VMEM((scen + 8, 128), F32),
            pltpu.VMEM((slices, scen + 8, 128), F32),
            pltpu.VMEM((8, 128), F32),
            pltpu.VMEM((units, 8, 128), F32),
            pltpu.VMEM((scen, 128), F32),
            pltpu.VMEM((scen, 128), F32),
            dma((slices,)), dma((slices,)), dma((units,)), dma((units,)),
            dma((2, items)), dma((2, items)), dma((2, items)), dma((2, items)),
            dma((items,)), dma((items,)), dma((items,)), dma((items,)),
        ],
        compiler_params=pltpu.CompilerParams(
            collective_id=0, has_side_effects=True, vmem_limit_bytes=48 * 1024 * 1024
        ),
        cost_estimate=pl.CostEstimate(
            flops=12 * scen * arcs * 128, bytes_accessed=8 * scen * arcs, transcendentals=0
        ),
    )(
        flow_start[0, 0], node_start[0, 0], seat_start[0], arc_cost.reshape(arc_blocks, 128),
        demand[0], seat_counts, tails, heads, targets, meta,
    )
    return flows[None, None], prices[None, None], seats[None]


def solution(mesh):
    shape = dict(mesh.shape)
    by_arc = P(("groups", "unit"), ("week", "region"), None, None)
    by_seat = P(("groups", "week", "region"), None, None)
    flat = P(("groups", "unit"), ("week", "region"), None)
    return jax.shard_map(
        functools.partial(local, shape["unit"], shape["week"]),
        mesh=mesh,
        in_specs=(
            by_arc, by_arc, by_seat, flat, by_seat, P(("groups", "unit")), flat, flat, flat,
        ),
        out_specs=(by_arc, by_arc, by_seat),
        check_vma=False,
    )
```

time: 218 us -> 93.3 us (0.43)
  Pallas kernels: 0 us -> 79.1 us
  matrix products: 68.8 us -> 0 us
  waiting for transfers between devices: 67.2 us -> 0 us
  blocking collectives: 39.2 us -> 0 us
  between operations: 15.9 us -> 1.31 us
  other arithmetic: 11.1 us -> 1.05 us
  starting transfers between devices: 5.55 us -> 0 us
    pallas_call x0 -> x1, Pallas kernels: none -> 79.1 us  [local(): pl.pallas_call(functools.partial(kernel, units, weeks, chunks), out_shape...]
    dot_general x24 -> x0, matrix products: 68.8 us -> none  [the longest x6 29.8 us: pick_values(): gathered = jnp.einsum('sbn,bkn->sbk', picked, within_hot, precision=HIGHEST)]
    psum x2 -> x0, waiting for transfers between devices: 64 us -> none  [local(): seat_total = lax.psum(seat_part, 'unit')]
    psum x2 -> x0, blocking collectives: 39.2 us -> none  [the longest x1 33.5 us: local(): cost_total = lax.psum(cost_squares, ('unit', 'week', 'region'))]
    ppermute x8 -> x0, starting transfers between devices: 5.29 us -> none  [the longest x4 4.63 us: from_behind(): lax.ppermute(x, axis, [(i, (i + by) % length) for i in range(length)])]
    broadcast_in_dim x2 -> x0, other arithmetic: 3.28 us -> none  [local(): return (flow_now[None, None], prices[None, None], covers[None])]
    ppermute x8 -> x0, waiting for transfers between devices: 3.14 us -> none  [the longest x4 3.13 us: from_behind(): lax.ppermute(x, axis, [(i, (i + by) % length) for i in range(length)])]
    unnamed x37 -> x17, local copies, waits for them, and re-layouts: 6.46 us -> 9.29 us
  transfers between devices with their start and end apart: 10 -> 0, of which waited for: 3 -> 0; matrix products, arithmetic and copies ran while one was open for 22% -> 0% of each run, Pallas kernels for 0% -> 0%
where the time goes in v1:
time: 93.3 us; the launch traced here: 92.6 us
  Pallas kernels  79.1 us (85%)
  local copies, waits for them, and re-layouts  11.1 us (12%)
  between operations  1.31 us (1%)
  other arithmetic  1.05 us (1%)
    pallas_call x1, Pallas kernels, local(): pl.pallas_call(functools.partial(kernel, units, weeks, chunks), out_shape...  79.1 us
    unnamed x17, local copies, waits for them, and re-layouts  9.29 us

profile of v1, /device:TPU:0, one launch (start us, length us, event | category | flops | bytes accessed | tf_op | source)
XLA Modules:
  0.0 92.6 jit_solution(1486046064478833477)
XLA Ops:
  1.3 0.9 slice_reduce_fusion
  2.1 0.9 slice_reduce_fusion.1
  3.0 0.8 fusion.1
  3.9 0.2 select_reduce_fusion
  4.1 0.1 concatenate.3.meta_ref
  4.2 0.0 copy-start
  4.2 1.2 %copy-done = f32[1,64,4096]{2,1,0:T(8,128)S(1)} copy-done((f32[1,64,4096]{2,1,0:T(8,128)S(1)}, f32[1,64,4096]{2,1,0:T(8,128)}, u32[]{:S(2)}) %copy-start) | copy-done | bytes 1048600
  5.4 0.0 copy-start.1
  5.4 1.2 %copy-done.1 = f32[1,64,4096]{2,1,0:T(8,128)S(1)} copy-done((f32[1,64,4096]{2,1,0:T(8,128)S(1)}, f32[1,64,4096]{2,1,0:T(8,128)}, u32[]{:S(2)}) %copy-start.1) | copy-done | bytes 1048600
  6.6 0.0 copy-start.2
  6.6 0.8 copy-done.2
  7.4 0.0 copy-start.3
  7.4 0.8 copy-done.3
  8.1 0.0 copy-start.4
  8.1 0.9 copy-done.4
  9.0 0.0 copy-start.5
  9.0 0.7 copy-done.5
  9.8 0.0 copy-start.6
  9.8 0.8 copy-done.6
  10.5 79.1 %shard_map.112 = (f32[64,8192]{1,0:T(8,128)S(1)}, f32[64,512]{1,0:T(8,128)S(1)}, f32[64,4096]{1,0:T(8,128)S(1)}) custom-call(f32[64,8192]{1,0:T(8,128)} %bitcast.24, f32[64,512]{1,0:T(8,128)S(1)} %bitcast.19, f32[64,4096]{1,0:T(8,128)S(1)} %bitcast.12, f32[64,128]{1,0:T(8,128)S(1)} %bitcast.23, f32[64,4096]{1,0:T(8,128)S(1)} %bitcast.13, ...), custom_call_target="tpu_custom_call" | custom-call | flops 805306368 | bytes 4194304 | tf_op jit(solution)/shard_map/pallas_call | solution.py:415
  89.6 1.3 %copy.16 = f32[1,1,64,8192]{3,2,1,0:T(8,128)} copy(f32[1,1,64,8192]{3,2,1,0:T(8,128)S(1)} %bitcast.11) | data formatting | bytes 4194304
  91.0 0.7 copy.17
  91.6 1.0 %copy.18 = f32[1,64,4096]{2,1,0:T(8,128)} copy(f32[1,64,4096]{2,1,0:T(8,128)S(1)} %bitcast.14) | data formatting | bytes 2097152
  (2 shorter events, 0.0 us)
Async XLA Ops:
  4.2 1.2 %copy-start = (f32[1,64,4096]{2,1,0:T(8,128)S(1)}, f32[1,64,4096]{2,1,0:T(8,128)}, u32[]{:S(2)}) copy-start(f32[1,64,4096]{2,1,0:T(8,128)} %param.11) | copy-start | bytes 3145732
  5.4 1.2 %copy-start.1 = (f32[1,64,4096]{2,1,0:T(8,128)S(1)}, f32[1,64,4096]{2,1,0:T(8,128)}, u32[]{:S(2)}) copy-start(f32[1,64,4096]{2,1,0:T(8,128)} %param.13) | copy-start | bytes 3145732
  6.6 0.8 copy-start.2
  7.4 0.8 copy-start.3
  8.1 0.9 copy-start.4
  9.0 0.7 copy-start.5
  9.8 0.8 copy-start.6

commit v2 on v1

--- a/solution.py
+++ b/solution.py
@@ -14,6 +14,9 @@
 STEP = 0.5
 CHUNKS = 4
 UNROLL = 8
+BATCH = 8
+PIECES = 4
+DIMS = (((1,), (1,)), ((), ()))
 MESH = pl.DeviceIdType.MESH
 F32 = jnp.float32
 BF16 = jnp.bfloat16
@@ -31,10 +34,11 @@
 
 def kernel(
     units, weeks, chunks,
-    flow_ref, node_ref, seat_ref, cost_ref, demand_ref, count_ref, tail_ref, head_ref, cover_ref,
+    flow_hbm, node_hbm, seat_hbm, cost_hbm, demand_hbm, count_ref, tail_hbm, head_hbm, cover_hbm,
     meta_ref,
     flow_out, node_out, seat_out,
-    hot_ends, hot_cover, covers, price_local, chain, own_price, recv_price, own_balance, send_in,
+    node_ref, seat_ref, cost_ref, demand_ref, tail_ref, head_ref, cover_ref, load_sem,
+    hot_ends, hot_cover, covers, price_local, spread, chain, own_price, recv_price, own_balance, send_in,
     recv_in, part, send_right, send_left, recv_right, recv_left, stat_mine, stat_slices, cost_mine,
     cost_units, primal, dual,
     stat_send, stat_recv, unit_send, unit_recv, price_send, price_recv, in_send, in_recv,
@@ -43,13 +47,14 @@
     me = lax.axis_index("unit")
     week = lax.axis_index("week")
     region = lax.axis_index("region")
-    scen, arcs = flow_ref.shape
+    scen, arcs = flow_out.shape
     nodes = node_ref.shape[1]
     trips = seat_ref.shape[1]
     rows = scen // chunks
     node_blocks = nodes // 128
     trip_blocks = trips // 128
     arc_blocks = arcs // 128
+    share = trip_blocks // PIECES
     cover_blocks = cover_ref.shape[0]
     slices = 2 * weeks
     mine = week * 2 + region
@@ -57,6 +62,19 @@
     behind = lax.rem(week + weeks - 1, weeks)
     stride = max(chunks, units - 1)
     scale = count_ref[0] / units
+
+    loads = [
+        pltpu.make_async_copy(source, target, load_sem.at[n])
+        for n, (source, target) in enumerate(
+            (
+                (demand_hbm, demand_ref), (cost_hbm, cost_ref), (node_hbm, node_ref),
+                (head_hbm, head_ref), (tail_hbm, tail_ref), (cover_hbm, cover_ref),
+                (seat_hbm, seat_ref), (flow_hbm, flow_out),
+            )
+        )
+    ]
+    for load in loads:
+        load.start()
 
     barrier = pltpu.get_barrier_semaphore()
     for step in range(1, units):
@@ -69,6 +87,8 @@
             device_id_type=MESH,
         )
 
+    for load in loads[0:3]:
+        load.wait()
     demand_squares = jnp.zeros((scen, 128), F32)
     for block in range(trip_blocks):
         piece = demand_ref[:, block * 128 : block * 128 + 128]
@@ -115,17 +135,19 @@
             device_id=target, device_id_type=MESH,
         )
 
-    def right_copy(item):
+    def right_copy(item, q):
+        some = pl.ds(q * share, share)
         return pltpu.make_async_remote_copy(
-            src_ref=send_right.at[item], dst_ref=recv_right.at[item],
-            send_sem=right_send.at[item], recv_sem=right_recv.at[item],
+            src_ref=send_right.at[item, some], dst_ref=recv_right.at[item, some],
+            send_sem=right_send.at[item, q], recv_sem=right_recv.at[item, q],
             device_id={"unit": lax.rem(me + 1, units)}, device_id_type=MESH,
         )
 
-    def left_copy(item):
+    def left_copy(item, q):
+        some = pl.ds(q * share, share)
         return pltpu.make_async_remote_copy(
-            src_ref=send_left.at[item], dst_ref=recv_left.at[item],
-            send_sem=left_send.at[item], recv_sem=left_recv.at[item],
+            src_ref=send_left.at[item, some], dst_ref=recv_left.at[item, some],
+            send_sem=left_send.at[item, q], recv_sem=left_recv.at[item, q],
             device_id={"unit": lax.rem(me + units - 1, units)}, device_id_type=MESH,
         )
 
@@ -134,6 +156,9 @@
     for c in range(chunks):
         price_copy(0, c).start()
         price_copy(1, c).start()
+
+    for load in loads[3:]:
+        load.wait()
 
     sub = lax.broadcasted_iota(jnp.int32, (128, 128), 0)
 
@@ -161,7 +186,6 @@
             covers[c * trip_blocks + block] = seat_ref[
                 c * rows : c * rows + rows, block * 128 : block * 128 + 128
             ]
-    flow_out[...] = flow_ref[...]
     chain[0] = jnp.zeros((rows, 128), F32)
 
     @pl.when(me == 0)
@@ -219,52 +243,61 @@
                 costs = cost_ref[at, :]
                 if with_cover:
                     targets = cover_ref[at, :] & 127
-                for k in range(UNROLL):
-                    b = base + k
-                    head_block = meta_ref[head_at + b]
-                    tail_block = meta_ref[tail_at + b]
-                    head_value = pick(
-                        price_local[side * node_blocks + head_block],
-                        jnp.broadcast_to(heads[k : k + 1, :], (rows, 128)),
-                    )
-                    tail_value = pick(
-                        price_local[tail_block],
-                        jnp.broadcast_to(tails[k : k + 1, :], (rows, 128)),
-                    )
-                    gradient = jnp.broadcast_to(costs[k : k + 1, :], (rows, 128))
+                for first_k in range(0, UNROLL, BATCH):
+                    batch = range(first_k, first_k + BATCH)
+                    head_block = [meta_ref[head_at + base + k] for k in batch]
+                    tail_block = [meta_ref[tail_at + base + k] for k in batch]
+                    column = [pl.ds(pl.multiple_of((base + k) * 128, 128), 128) for k in batch]
+                    head_price = [price_local[side * node_blocks + m] for m in head_block]
+                    tail_price = [price_local[m] for m in tail_block]
+                    now = [flow_out[there, at] for at in column]
                     if with_cover:
-                        seat = pick(
-                            covers[c * trip_blocks + meta_ref[cover_at + b]],
-                            jnp.broadcast_to(targets[k : k + 1, :], (rows, 128)),
+                        cover_price = [
+                            covers[c * trip_blocks + meta_ref[cover_at + base + k]] for k in batch
+                        ]
+                    updated, halves = [], []
+                    for n, k in enumerate(batch):
+                        wide = lambda row: jnp.broadcast_to(row[k : k + 1, :], (rows, 128))
+                        gradient = wide(costs)
+                        if with_cover:
+                            gradient = gradient - scale * pick(cover_price[n], wide(targets))
+                        gradient = gradient - (
+                            pick(head_price[n], wide(heads)) - pick(tail_price[n], wide(tails))
                         )
-                        gradient = gradient - scale * seat
-                    gradient = gradient - (head_value - tail_value)
-                    column = pl.ds(pl.multiple_of(b * 128, 128), 128)
-                    now = flow_out[there, column]
-                    updated = jnp.maximum(now - step_size * gradient, 0.0)
-                    flow_out[there, column] = updated
-                    halves = split_rows(2.0 * updated - now)
-                    ends = lax.dot_general(
-                        halves, hot_ends[b], (((1,), (1,)), ((), ())),
-                        preferred_element_type=F32,
-                    )
-                    ends = ends[0:rows] + ends[rows : 2 * rows]
-                    into, outof = ends[:, 0:128], ends[:, 128:256]
-                    for m in range(node_blocks):
-                        landed = jnp.where(head_block == m, into, 0.0)
-                        left = jnp.where(tail_block == m, outof, 0.0)
-                        if side == 0:
-                            own[m] = own[m] + (landed - left)
-                        else:
-                            own[m] = own[m] - left
-                            away[m] = away[m] + landed
+                        updated.append(jnp.maximum(now[n] - step_size * gradient, 0.0))
+                        halves.append(split_rows(2.0 * updated[n] - now[n]))
+                    tables = [hot_ends[base + k] for k in batch]
+                    ends = [
+                        lax.dot_general(
+                            halves[n], tables[n], DIMS, preferred_element_type=F32
+                        )
+                        for n in range(BATCH)
+                    ]
                     if with_cover:
-                        filled = lax.dot_general(
-                            halves, hot_cover[b], (((1,), (1,)), ((), ())),
-                            preferred_element_type=F32,
-                        )
-                        filled = filled[0:rows] + filled[rows : 2 * rows]
-                        chain[b + 1] = scale * filled + chain[meta_ref[prev_at + b]]
+                        filled = [
+                            lax.dot_general(
+                                halves[n], hot_cover[base + k], DIMS, preferred_element_type=F32
+                            )
+                            for n, k in enumerate(batch)
+                        ]
+                    for n in range(BATCH):
+                        flow_out[there, column[n]] = updated[n]
+                    for n in range(BATCH):
+                        total = ends[n][0:rows] + ends[n][rows : 2 * rows]
+                        into, outof = total[:, 0:128], total[:, 128:256]
+                        for m in range(node_blocks):
+                            landed = jnp.where(head_block[n] == m, into, 0.0)
+                            left = jnp.where(tail_block[n] == m, outof, 0.0)
+                            if side == 0:
+                                own[m] = own[m] + (landed - left)
+                            else:
+                                own[m] = own[m] - left
+                                away[m] = away[m] + landed
+                    if with_cover:
+                        for n, k in enumerate(batch):
+                            spread[base + k] = scale * (
+                                filled[n][0:rows] + filled[n][rows : 2 * rows]
+                            )
                 return tuple(own), tuple(away)
 
             return lax.fori_loop(0, (end - first) // UNROLL, body, start)
@@ -280,6 +313,8 @@
             send_in[1, item, m] = away_other[m]
         in_copy(0, item).start()
         in_copy(1, item).start()
+        for b in range(cover_blocks):
+            chain[b + 1] = spread[b] + chain[meta_ref[prev_at + b]]
         for m in range(trip_blocks):
             part[item, m] = chain[meta_ref[last_at + m]]
 
@@ -334,34 +369,39 @@
         def _():
             action(it * chunks + c, c, it)
 
-    def forward_right(item, c, it):
+    def forward_right(q, item, c, it):
+        some = pl.ds(q * share, share)
+
         @pl.when(me > 0)
         def _():
-            right_copy(item).wait_recv()
+            right_copy(item, q).wait_recv()
 
         @pl.when(me < units - 1)
         def _():
-            send_right[item] = part[item] + recv_right[item]
-            right_copy(item).start()
-
-    def forward_left(item, c, it):
+            send_right[item, some] = part[item, some] + recv_right[item, some]
+            right_copy(item, q).start()
+
+    def forward_left(q, item, c, it):
+        some = pl.ds(q * share, share)
+
         @pl.when(me < units - 1)
         def _():
-            left_copy(item).wait_recv()
+            left_copy(item, q).wait_recv()
 
         @pl.when(me > 0)
         def _():
-            send_left[item] = part[item] + recv_left[item]
-            left_copy(item).start()
+            send_left[item, some] = part[item, some] + recv_left[item, some]
+            left_copy(item, q).start()
 
     far = jnp.maximum(me, units - 1 - me)
 
     @pl.loop(0, (ITERS - 1) * stride + chunks + units - 1)
     def _(slot):
         at_slot(slot, lambda item, c, it: compute(item, c))
-        at_slot(slot - me, forward_right)
-        at_slot(slot - (units - 1 - me), forward_left)
-        at_slot(slot, settle_nodes)
+        at_slot(slot - 1, settle_nodes)
+        for q in range(PIECES):
+            at_slot(slot - me, functools.partial(forward_right, q))
+            at_slot(slot - (units - 1 - me), functools.partial(forward_left, q))
         at_slot(slot - far, settle_seats)
 
     for step in range(1, slices):
@@ -377,11 +417,13 @@
 
         @pl.when(me < units - 1)
         def _():
-            right_copy(item).wait_send()
+            for q in range(PIECES):
+                right_copy(item, q).wait_send()
 
         @pl.when(me > 0)
         def _():
-            left_copy(item).wait_send()
+            for q in range(PIECES):
+                left_copy(item, q).wait_send()
 
 
 def local(
@@ -411,6 +453,7 @@
     slices = 2 * weeks
     vmem = pl.BlockSpec(memory_space=pltpu.VMEM)
     smem = pl.BlockSpec(memory_space=pltpu.SMEM)
+    hbm = pl.BlockSpec(memory_space=pltpu.HBM)
     dma = pltpu.SemaphoreType.DMA
     flows, prices, seats = pl.pallas_call(
         functools.partial(kernel, units, weeks, chunks),
@@ -419,13 +462,22 @@
             jax.ShapeDtypeStruct((scen, nodes), F32),
             jax.ShapeDtypeStruct((scen, trips), F32),
         ),
-        in_specs=[vmem, vmem, vmem, vmem, vmem, smem, vmem, vmem, vmem, smem],
+        in_specs=[hbm, hbm, hbm, hbm, hbm, smem, hbm, hbm, hbm, smem],
         out_specs=(vmem, vmem, vmem),
         scratch_shapes=[
+            pltpu.VMEM((scen, nodes), F32),
+            pltpu.VMEM((scen, trips), F32),
+            pltpu.VMEM((arc_blocks, 128), F32),
+            pltpu.VMEM((scen, trips), F32),
+            pltpu.VMEM((arc_blocks, 128), jnp.int32),
+            pltpu.VMEM((arc_blocks, 128), jnp.int32),
+            pltpu.VMEM((cover_blocks, 128), jnp.int32),
+            dma((8,)),
             pltpu.VMEM((arc_blocks, 256, 128), BF16),
             pltpu.VMEM((cover_blocks, 128, 128), BF16),
             pltpu.VMEM((chunks * trip_blocks, rows, 128), F32),
             pltpu.VMEM((3 * node_blocks, rows, 128), F32),
+            pltpu.VMEM((cover_blocks, rows, 128), F32),
             pltpu.VMEM((cover_blocks + 1, rows, 128), F32),
             pltpu.VMEM((items, node_blocks, rows, 128), F32),
             pltpu.VMEM((2, items, node_blocks, rows, 128), F32),
@@ -443,10 +495,10 @@
             pltpu.VMEM((scen, 128), F32),
             dma((slices,)), dma((slices,)), dma((units,)), dma((units,)),
             dma((2, items)), dma((2, items)), dma((2, items)), dma((2, items)),
-            dma((items,)), dma((items,)), dma((items,)), dma((items,)),
+            dma((items, PIECES)), dma((items, PIECES)), dma((items, PIECES)), dma((items, PIECES)),
         ],
         compiler_params=pltpu.CompilerParams(
-            collective_id=0, has_side_effects=True, vmem_limit_bytes=48 * 1024 * 1024
+            collective_id=0, has_side_effects=True, vmem_limit_bytes=62 * 1024 * 1024
         ),
         cost_estimate=pl.CostEstimate(
             flops=12 * scen * arcs * 128, bytes_accessed=8 * scen * arcs, transcendentals=0

time: 93.3 us -> 86.2 us (0.924)
  local copies, waits for them, and re-layouts: 11.1 us -> 7.18 us
  Pallas kernels: 79.1 us -> 76.3 us
    unnamed x17 -> x7, local copies, waits for them, and re-layouts: 9.29 us -> 4.79 us
    pallas_call x1, Pallas kernels: 79.1 us -> 76.3 us  [local(): pl.pallas_call(functools.partial(kernel, units, weeks, chunks), out_shape...]
where the time goes in v2:
time: 86.2 us; the launch traced here: 85.8 us
  Pallas kernels  76.3 us (89%)
  local copies, waits for them, and re-layouts  7.18 us (8%)
  between operations  1.32 us (2%)
  other arithmetic  1.05 us (1%)
    pallas_call x1, Pallas kernels, local(): pl.pallas_call(functools.partial(kernel, units, weeks, chunks), out_shape...  76.3 us
    unnamed x7, local copies, waits for them, and re-layouts  4.79 us

profile of v2, /device:TPU:0, one launch (start us, length us, event | category | flops | bytes accessed | tf_op | source)
XLA Modules:
  0.0 85.8 jit_solution(2585327816135644388)
XLA Ops:
  1.3 0.9 %slice_reduce_fusion = s32[64]{0:T(128)S(1)} fusion(s32[64,128]{1,0:T(8,128)} %bitcast.16), kind=kLoop, calls=%fused_computation | loop fusion | bytes 512 | tf_op jit(solution)/shard_map/slice | solution.py:448
  2.1 0.9 %slice_reduce_fusion.1 = s32[64]{0:T(128)S(1)} fusion(s32[64,128]{1,0:T(8,128)} %bitcast.18), kind=kLoop, calls=%fused_computation.1 | loop fusion | bytes 512 | tf_op jit(solution)/shard_map/slice | solution.py:448
  3.0 0.8 fusion.1
  3.9 0.2 select_reduce_fusion
  4.1 0.7 concatenate.3.meta_ref
  4.7 76.3 %shard_map.112 = (f32[64,8192]{1,0:T(8,128)}, f32[64,512]{1,0:T(8,128)}, f32[64,4096]{1,0:T(8,128)}) custom-call(f32[64,8192]{1,0:T(8,128)} %bitcast.11, f32[64,512]{1,0:T(8,128)} %bitcast.20, f32[64,4096]{1,0:T(8,128)} %bitcast.13, f32[64,128]{1,0:T(8,128)} %bitcast.24, f32[64,4096]{1,0:T(8,128)} %bitcast.14, f32[1]{0:T(128)S(6)} %copy.15.count_ref, ...), custom_call_target="tpu_custom_call" | custom-call | flops 805306368 | bytes 4194304 | tf_op jit(solution)/shard_map/pallas_call | solution.py:458
  81.0 0.0 copy-start.1
  81.0 0.0 copy-start
  81.0 3.2 %copy.16 = f32[1,1,64,8192]{3,2,1,0:T(8,128)} copy(f32[1,1,64,8192]{3,2,1,0:T(8,128)} %bitcast.12) | data formatting | bytes 4194304
  84.2 0.0 copy-done.1
  84.2 0.7 copy.17
  84.9 0.0 copy-done
  84.9 1.0 %copy.18 = f32[1,64,4096]{2,1,0:T(8,128)} copy(f32[1,64,4096]{2,1,0:T(8,128)S(1)} %bitcast.15) | data formatting | bytes 2097152
  (2 shorter events, 0.0 us)
Async XLA Ops:
  81.0 3.2 %copy-start.1 = (f32[64,512]{1,0:T(8,128)S(1)}, f32[64,512]{1,0:T(8,128)}, u32[]{:S(2)}) copy-start(f32[64,512]{1,0:T(8,128)} %get-tuple-element.7) | copy-start | bytes 393220
  81.0 3.8 %copy-start = (f32[64,4096]{1,0:T(8,128)S(1)}, f32[64,4096]{1,0:T(8,128)}, u32[]{:S(2)}) copy-start(f32[64,4096]{1,0:T(8,128)} %get-tuple-element.8) | copy-start | bytes 3145732
